TPU v7x, 32 devices: a whole 2x2x4 slice. The times are simulated.
32 devices in a mesh: batch: 4 (over z), seq: 8 (over y, x, core).
Axes of the slice: x: 2, y: 2, z: 4, core: 2. Of those that a mesh axis runs over, the one named last changes fastest.
Arguments:
- tokens: bfloat16 [8, 4096, 768], P('batch', 'seq'), may hold values from -6 to 6
- sequence_lengths: int32 [8, 4], P('batch'), may hold values from 0 to 4096, as said below
- norm_gains: bfloat16 [2, 768], P(None, ('batch', 'seq')), may hold values from 0.099609375 to 1.8984375
- norm_shifts: bfloat16 [2, 768], P(None, ('batch', 'seq')), may hold values from -4 to 4
- mixing_weight: bfloat16 [768, 2304], P(('batch', 'seq')), may hold values from -0.21875 to 0.21875
- mixing_offset: bfloat16 [2304], P(('batch', 'seq')), may hold values from -1.5 to 1.5
- feature_maps: bfloat16 [768, 128], P(('batch', 'seq')), may hold values from -4 to 4
- output_weight: bfloat16 [768, 768], P(('batch', 'seq')), may hold values from -0.875 to 0.875
- branch_offsets: bfloat16 [2, 768], P(None, ('batch', 'seq')), may hold values from -4 to 4
- expand_weight: bfloat16 [768, 3072], P(('batch', 'seq')), may hold values from -0.21875 to 0.21875
- hidden_offset: bfloat16 [3072], P(('batch', 'seq')), may hold values from -4 to 4
- shrink_weight: bfloat16 [3072, 768], P(('batch', 'seq')), may hold values from -0.109375 to 0.109375
- cotangent: bfloat16 [8, 4096, 768], P('batch', 'seq'), may hold values from -6 to 6
Outputs:
- layer_output: bfloat16 [8, 4096, 768], P('batch', 'seq')
- input_gradient: bfloat16 [8, 4096, 768], P('batch', 'seq')
- gains_gradient: float32 [2, 768], P(None, ('batch', 'seq'))
- shifts_gradient: float32 [2, 768], P(None, ('batch', 'seq'))
- mixing_gradient: float32 [768, 2304], P(('batch', 'seq'))
- offset_gradient: float32 [2304], P(('batch', 'seq'))
- feature_gradient: float32 [768, 128], P(('batch', 'seq'))
- output_gradient: float32 [768, 768], P(('batch', 'seq'))
- branch_gradient: float32 [2, 768], P(None, ('batch', 'seq'))
- expand_gradient: float32 [768, 3072], P(('batch', 'seq'))
- hidden_gradient: float32 [3072], P(('batch', 'seq'))
- shrink_gradient: float32 [3072, 768], P(('batch', 'seq'))
Inputs may be any that keep to these rules, and one draw needn't show every extreme that they name: `sequence_lengths`: each row lists its sequences' lengths in order, then zeros; the lengths sum to 4096 and each is 1024 or more and under 3 * 1024, except that among the 2 rows of each index of batch one row is a single sequence of 4096.
All inputs are finite; a program needn't handle non-finite values.
Results may differ from a plain program's by a relative error of at most 0.015.
Values may be sent and summed in bfloat16 or wider, within the bound.
No kernel may reach another device: no remote copies, remote signals or barrier semaphores. Data moves between devices by JAX's collectives and lax.ppermute only.
A program may use at most 256 MiB of HBM per device.

v0:
```python
import jax
import jax.numpy as jnp
from jax import lax
from jax.sharding import PartitionSpec as P

HD = 64


EPSILON = 1e-05
PRECISE = lax.Precision.HIGHEST


def carried_in(value, axis, combine, identity, reverse):
    size, mine = (lax.axis_size(axis), lax.axis_index(axis))
    everything = jax.tree.map(
        lambda part, kind: lax.all_gather(part.astype(kind), axis),
        value,
        (jnp.bfloat16, jnp.bfloat16, jnp.bfloat16),
    )
    start = jax.tree.map(
        lambda part, zero: jnp.broadcast_to(jnp.asarray(zero, part.dtype), part.shape),
        value,
        identity,
    )

    def turn(k, before):
        at = size - 1 - k if reverse else k
        reached = at > mine if reverse else at < mine
        new = combine(
            before, jax.tree.map(lambda part, own: part[at].astype(own.dtype), everything, value)
        )
        return jax.tree.map(lambda a, b: jnp.where(reached, a, b), new, before)

    return lax.fori_loop(0, size, turn, start)


def layer_norm(values, gain_row, shift_row):
    center = jnp.mean(values, axis=-1, keepdims=True)
    centered = values - center
    spread = jnp.mean(centered * centered, axis=-1, keepdims=True)
    return centered * lax.rsqrt(spread + EPSILON) * gain_row + shift_row


def feature_map(logits):
    return jnp.concatenate(
        [jax.nn.softmax(logits, axis=-1), jax.nn.softmax(-logits, axis=-1)], axis=-1
    )


def activation(values):
    return jax.nn.gelu(values, approximate=True)


def combine(earlier, later):
    retained = 1.0 - later[2]
    return (
        later[0] + retained[:, None, None, None] * earlier[0],
        later[1] + retained[:, None, None] * earlier[1],
        jnp.maximum(earlier[2], later[2]),
    )


def local(
    tokens,
    sequence_lengths,
    norm_gains,
    norm_shifts,
    mixing_weight,
    mixing_offset,
    feature_maps,
    output_weight,
    branch_offsets,
    expand_weight,
    hidden_offset,
    shrink_weight,
    cotangent,
):
    gathered = (
        lax.all_gather(norm_gains, ("batch", "seq"), axis=1, tiled=True),
        lax.all_gather(norm_shifts, ("batch", "seq"), axis=1, tiled=True),
        lax.all_gather(mixing_weight, ("batch", "seq"), axis=0, tiled=True),
        lax.all_gather(mixing_offset, ("batch", "seq"), axis=0, tiled=True),
        lax.all_gather(feature_maps, ("batch", "seq"), axis=0, tiled=True),
        lax.all_gather(output_weight, ("batch", "seq"), axis=0, tiled=True),
        lax.all_gather(branch_offsets, ("batch", "seq"), axis=1, tiled=True),
        lax.all_gather(expand_weight, ("batch", "seq"), axis=0, tiled=True),
        lax.all_gather(hidden_offset, ("batch", "seq"), axis=0, tiled=True),
        lax.all_gather(shrink_weight, ("batch", "seq"), axis=0, tiled=True),
    )
    (
        gain_rows,
        shift_rows,
        mixing,
        offset_mix,
        maps,
        out_weight,
        branch_rows,
        expand,
        hidden_bias,
        shrink,
    ) = gathered
    row_count, tok_count, model_width = tokens.shape
    head_count = model_width // HD
    places = lax.axis_index("seq") * tok_count + jnp.arange(tok_count, dtype=jnp.int32)
    starts = jnp.cumsum(sequence_lengths, axis=1) - sequence_lengths
    doc_ids = jnp.sum((starts[:, None, :] <= places[None, :, None]).astype(jnp.int32), axis=2)
    before = jnp.sum((starts <= places[0] - 1).astype(jnp.int32), axis=1)
    carry_mask = (doc_ids == before[:, None]).astype(jnp.float32)
    last_mask = (doc_ids == doc_ids[:, -1:]).astype(jnp.float32)
    restart = (doc_ids[:, -1] != before).astype(jnp.float32)
    causal = jnp.arange(tok_count)[None, :] <= jnp.arange(tok_count)[:, None]
    allowed = ((doc_ids[:, :, None] == doc_ids[:, None, :]) & causal[None]).astype(jnp.float32)
    allowed_low = allowed.astype(jnp.bfloat16)
    carry_low = carry_mask.astype(jnp.bfloat16)
    last_low = last_mask.astype(jnp.bfloat16)
    inputs = tokens.astype(jnp.float32)
    normed_full, norm_in_back = jax.vjp(
        layer_norm, inputs, gain_rows[0].astype(jnp.float32), shift_rows[0].astype(jnp.float32)
    )
    normed_in = normed_full.astype(jnp.bfloat16)
    projected = (
        jnp.einsum("rtd,de->rte", normed_in, mixing, preferred_element_type=jnp.float32)
        + offset_mix.astype(jnp.float32)
    ).astype(jnp.bfloat16)
    separated = projected.reshape(row_count, tok_count, 3, head_count, HD)
    queries = separated[:, :, 0]
    keys_all = separated[:, :, 1]
    values = separated[:, :, 2]
    layout = maps.reshape(head_count, HD, 2, HD)
    query_logits = jnp.einsum(
        "rthd,hde->rthe", queries, layout[:, :, 0], preferred_element_type=jnp.float32
    )
    key_logits = jnp.einsum(
        "rthd,hde->rthe", keys_all, layout[:, :, 1], preferred_element_type=jnp.float32
    )
    phi_query_full, query_map_back = jax.vjp(feature_map, query_logits)
    phi_key_full, key_map_back = jax.vjp(feature_map, key_logits)
    phi_query = phi_query_full.astype(jnp.bfloat16)
    phi_key = phi_key_full.astype(jnp.bfloat16)
    state_sum = jnp.einsum(
        "rthf,rthe->rhfe",
        phi_key * last_low[:, :, None, None],
        values,
        preferred_element_type=jnp.float32,
    )
    key_sum = jnp.einsum("rthf,rt->rhf", phi_key, last_low, preferred_element_type=jnp.float32)
    memory, key_memory, _ = carried_in(
        (state_sum, key_sum, restart),
        "seq",
        combine,
        (jnp.zeros_like(state_sum), jnp.zeros_like(key_sum), jnp.zeros_like(restart)),
        False,
    )
    query_heads = jnp.moveaxis(phi_query, 2, 0)
    key_heads = jnp.moveaxis(phi_key, 2, 0)
    value_heads = jnp.moveaxis(values, 2, 0)
    memory_heads = jnp.moveaxis(memory, 1, 0)
    key_memory_heads = jnp.moveaxis(key_memory, 1, 0)

    def head_forward(pieces):
        query_head, key_head, value_head, memory_head, key_memory_head = pieces
        scores = (
            jnp.einsum("rif,rjf->rij", query_head, key_head, preferred_element_type=jnp.float32)
            * allowed
        )
        denominator = jnp.sum(scores, axis=2) + carry_mask * jnp.einsum(
            "rif,rf->ri",
            query_head,
            key_memory_head,
            precision=PRECISE,
            preferred_element_type=jnp.float32,
        )
        numerator = jnp.einsum(
            "rij,rje->rie",
            scores.astype(jnp.bfloat16),
            value_head,
            preferred_element_type=jnp.float32,
        ) + carry_mask[:, :, None] * jnp.einsum(
            "rif,rfe->rie",
            query_head,
            memory_head,
            precision=PRECISE,
            preferred_element_type=jnp.float32,
        )
        return (numerator / denominator[:, :, None], denominator)

    attended_heads, denominators = lax.map(
        head_forward, (query_heads, key_heads, value_heads, memory_heads, key_memory_heads)
    )
    attended = (
        jnp.moveaxis(attended_heads, 0, 2)
        .reshape(row_count, tok_count, model_width)
        .astype(jnp.bfloat16)
    )
    branch = jnp.einsum(
        "rti,io->rto", attended, out_weight, preferred_element_type=jnp.float32
    ) + branch_rows[0].astype(jnp.float32)
    middle = inputs + branch
    mid_full, norm_mid_back = jax.vjp(
        layer_norm, middle, gain_rows[1].astype(jnp.float32), shift_rows[1].astype(jnp.float32)
    )
    normed_mid = mid_full.astype(jnp.bfloat16)
    preact = jnp.einsum(
        "rtd,df->rtf", normed_mid, expand, preferred_element_type=jnp.float32
    ) + hidden_bias.astype(jnp.float32)
    hidden_full, gelu_back = jax.vjp(activation, preact)
    hidden = hidden_full.astype(jnp.bfloat16)
    layer_output = (
        middle
        + jnp.einsum("rtf,fd->rtd", hidden, shrink, preferred_element_type=jnp.float32)
        + branch_rows[1].astype(jnp.float32)
    ).astype(jnp.bfloat16)
    mixing, maps, out_weight, expand, shrink = (
        lax.all_gather(mixing_weight, ("batch", "seq"), axis=0, tiled=True),
        lax.all_gather(feature_maps, ("batch", "seq"), axis=0, tiled=True),
        lax.all_gather(output_weight, ("batch", "seq"), axis=0, tiled=True),
        lax.all_gather(expand_weight, ("batch", "seq"), axis=0, tiled=True),
        lax.all_gather(shrink_weight, ("batch", "seq"), axis=0, tiled=True),
    )
    back_layout = maps.reshape(head_count, HD, 2, HD)
    upstream = cotangent.astype(jnp.float32)
    shrink_grad_sum = jnp.einsum(
        "rtf,rtd->fd", hidden, cotangent, preferred_element_type=jnp.float32
    )
    shrink_bias_sum = jnp.sum(upstream, axis=(0, 1))
    hidden_back = jnp.einsum("rtd,fd->rtf", cotangent, shrink, preferred_element_type=jnp.float32)
    preact_back = gelu_back(hidden_back)[0].astype(jnp.bfloat16)
    expand_grad_sum = jnp.einsum(
        "rtd,rtf->df", normed_mid, preact_back, preferred_element_type=jnp.float32
    )
    hidden_bias_sum = jnp.sum(preact_back, axis=(0, 1), dtype=jnp.float32)
    normed_mid_back = jnp.einsum(
        "rtf,df->rtd", preact_back, expand, preferred_element_type=jnp.float32
    )
    mid_norm_back, gain_mid_sum, shift_mid_sum = norm_mid_back(normed_mid_back)
    middle_back = upstream + mid_norm_back
    branch_back = middle_back.astype(jnp.bfloat16)
    output_grad_sum = jnp.einsum(
        "rti,rto->io", attended, branch_back, preferred_element_type=jnp.float32
    )
    output_bias_sum = jnp.sum(branch_back, axis=(0, 1), dtype=jnp.float32)
    attended_back = jnp.einsum(
        "rto,io->rti", branch_back, out_weight, preferred_element_type=jnp.float32
    )
    attended_back = jnp.moveaxis(attended_back.reshape(row_count, tok_count, head_count, HD), 2, 0)
    numerator_back = (attended_back / denominators[..., None]).astype(jnp.bfloat16)
    denominator_back = -jnp.sum(attended_back * attended_heads, axis=-1) / denominators
    state_local = jnp.einsum(
        "hrif,hrie->rhfe",
        query_heads * carry_low[None, :, :, None],
        numerator_back,
        preferred_element_type=jnp.float32,
    )
    key_local = jnp.einsum(
        "hrif,hri->rhf",
        query_heads,
        denominator_back * carry_mask[None],
        precision=PRECISE,
        preferred_element_type=jnp.float32,
    )
    state_back, key_back, _ = carried_in(
        (state_local, key_local, restart),
        "seq",
        combine,
        (jnp.zeros_like(state_local), jnp.zeros_like(key_local), jnp.zeros_like(restart)),
        True,
    )
    state_back_heads = jnp.moveaxis(state_back, 1, 0)
    key_back_heads = jnp.moveaxis(key_back, 1, 0)

    def head_backward(pieces):
        (
            query_head,
            key_head,
            value_head,
            memory_head,
            key_memory_head,
            numer_head,
            denom_head,
            state_head,
            key_state_head,
        ) = pieces
        scores = (
            jnp.einsum("rif,rjf->rij", query_head, key_head, preferred_element_type=jnp.float32)
            * allowed
        )
        scores_low = scores.astype(jnp.bfloat16)
        scores_back = (
            jnp.einsum("rie,rje->rij", numer_head, value_head, preferred_element_type=jnp.float32)
            + denom_head[:, :, None]
        ).astype(jnp.bfloat16) * allowed_low
        query_feat = jnp.einsum(
            "rij,rjf->rif", scores_back, key_head, preferred_element_type=jnp.float32
        ) + carry_mask[:, :, None] * (
            jnp.einsum(
                "rie,rfe->rif",
                numer_head,
                memory_head,
                precision=PRECISE,
                preferred_element_type=jnp.float32,
            )
            + denom_head[:, :, None] * key_memory_head[:, None, :]
        )
        key_feat = jnp.einsum(
            "rij,rif->rjf", scores_back, query_head, preferred_element_type=jnp.float32
        ) + last_mask[:, :, None] * (
            jnp.einsum(
                "rje,rfe->rjf",
                value_head,
                state_head,
                precision=PRECISE,
                preferred_element_type=jnp.float32,
            )
            + key_state_head[:, None, :]
        )
        value_feat = jnp.einsum(
            "rij,rie->rje", scores_low, numer_head, preferred_element_type=jnp.float32
        ) + last_mask[:, :, None] * jnp.einsum(
            "rjf,rfe->rje",
            key_head,
            state_head,
            precision=PRECISE,
            preferred_element_type=jnp.float32,
        )
        return (query_feat, key_feat, value_feat)

    query_feat_back, key_feat_back, values_back = lax.map(
        head_backward,
        (
            query_heads,
            key_heads,
            value_heads,
            memory_heads,
            key_memory_heads,
            numerator_back,
            denominator_back,
            state_back_heads,
            key_back_heads,
        ),
    )
    query_logits_back = query_map_back(jnp.moveaxis(query_feat_back, 0, 2))[0].astype(jnp.bfloat16)
    key_logits_back = key_map_back(jnp.moveaxis(key_feat_back, 0, 2))[0].astype(jnp.bfloat16)
    query_map_sum = jnp.einsum(
        "rthd,rthe->hde", queries, query_logits_back, preferred_element_type=jnp.float32
    )
    key_map_sum = jnp.einsum(
        "rthd,rthe->hde", keys_all, key_logits_back, preferred_element_type=jnp.float32
    )
    feature_grad_sum = jnp.stack([query_map_sum, key_map_sum], axis=2).reshape(model_width, 2 * HD)
    queries_back = jnp.einsum(
        "rthe,hde->rthd",
        query_logits_back,
        back_layout[:, :, 0],
        preferred_element_type=jnp.float32,
    )
    keys_back = jnp.einsum(
        "rthe,hde->rthd", key_logits_back, back_layout[:, :, 1], preferred_element_type=jnp.float32
    )
    projected_back = (
        jnp.stack([queries_back, keys_back, jnp.moveaxis(values_back, 0, 2)], axis=2)
        .reshape(row_count, tok_count, 3 * model_width)
        .astype(jnp.bfloat16)
    )
    mixing_grad_sum = jnp.einsum(
        "rtd,rte->de", normed_in, projected_back, preferred_element_type=jnp.float32
    )
    offset_grad_sum = jnp.sum(projected_back, axis=(0, 1), dtype=jnp.float32)
    normed_in_back = jnp.einsum(
        "rte,de->rtd", projected_back, mixing, preferred_element_type=jnp.float32
    )
    in_norm_back, gain_in_sum, shift_in_sum = norm_in_back(normed_in_back)
    input_gradient = (middle_back + in_norm_back).astype(jnp.bfloat16)
    gains_sum = jnp.stack([gain_in_sum, gain_mid_sum])
    shifts_sum = jnp.stack([shift_in_sum, shift_mid_sum])
    branch_sum = jnp.stack([output_bias_sum, shrink_bias_sum])
    summed = (
        lax.psum_scatter(gains_sum, ("batch", "seq"), scatter_dimension=1, tiled=True),
        lax.psum_scatter(shifts_sum, ("batch", "seq"), scatter_dimension=1, tiled=True),
        lax.psum_scatter(mixing_grad_sum, ("batch", "seq"), scatter_dimension=0, tiled=True),
        lax.psum_scatter(offset_grad_sum, ("batch", "seq"), scatter_dimension=0, tiled=True),
        lax.psum_scatter(feature_grad_sum, ("batch", "seq"), scatter_dimension=0, tiled=True),
        lax.psum_scatter(output_grad_sum, ("batch", "seq"), scatter_dimension=0, tiled=True),
        lax.psum_scatter(branch_sum, ("batch", "seq"), scatter_dimension=1, tiled=True),
        lax.psum_scatter(expand_grad_sum, ("batch", "seq"), scatter_dimension=0, tiled=True),
        lax.psum_scatter(hidden_bias_sum, ("batch", "seq"), scatter_dimension=0, tiled=True),
        lax.psum_scatter(shrink_grad_sum, ("batch", "seq"), scatter_dimension=0, tiled=True),
    )
    (
        gains_gradient,
        shifts_gradient,
        mixing_gradient,
        offset_gradient,
        feature_gradient,
        output_gradient,
        branch_gradient,
        expand_gradient,
        hidden_gradient,
        shrink_gradient,
    ) = summed
    return (
        layer_output,
        input_gradient,
        gains_gradient,
        shifts_gradient,
        mixing_gradient,
        offset_gradient,
        feature_gradient,
        output_gradient,
        branch_gradient,
        expand_gradient,
        hidden_gradient,
        shrink_gradient,
    )


def solution(mesh):
    placed = (
        P("batch", "seq", None),
        P("batch", None),
        P(None, ("batch", "seq")),
        P(None, ("batch", "seq")),
        P(("batch", "seq"), None),
        P(("batch", "seq")),
        P(("batch", "seq"), None),
        P(("batch", "seq"), None),
        P(None, ("batch", "seq")),
        P(("batch", "seq"), None),
        P(("batch", "seq")),
        P(("batch", "seq"), None),
        P("batch", "seq", None),
    )
    return jax.shard_map(
        local,
        mesh=mesh,
        in_specs=placed,
        out_specs=(
            P("batch", "seq", None),
            P("batch", "seq", None),
            P(None, ("batch", "seq")),
            P(None, ("batch", "seq")),
            P(("batch", "seq"), None),
            P(("batch", "seq")),
            P(("batch", "seq"), None),
            P(("batch", "seq"), None),
            P(None, ("batch", "seq")),
            P(("batch", "seq"), None),
            P(("batch", "seq")),
            P(("batch", "seq"), None),
        ),
        check_vma=False,
    )
```

profile of v0, /device:TPU:0, one launch (start us, length us, event | category | flops | bytes accessed | tf_op | source)
XLA Modules:
  0.0 1224.1 jit_solution(4773709378903862567)
XLA Ops:
  8.0 43.3 %all-gather.4 = bf16[32,24,2]{1,2,0:T(2,128)(2,1)S(1)} all-gather(bf16[1,24,2]{1,2,0:T(2,128)(2,1)} %bitcast.446), channel_id=1, replica_groups=mesh['batch'=4,'seq'=8] {'batch','seq'}, dimensions={0}, use_global_device_ids=true | all-gather | bytes 3168 | tf_op jit(solution)/shard_map/all_gather | solution.py:79
  51.4 36.8 %all-gather.5 = bf16[32,24,2]{1,2,0:T(2,128)(2,1)S(1)} all-gather(bf16[1,24,2]{1,2,0:T(2,128)(2,1)} %bitcast.447), channel_id=1, replica_groups=mesh['batch'=4,'seq'=8] {'batch','seq'}, dimensions={0}, use_global_device_ids=true | all-gather | bytes 3168 | tf_op jit(solution)/shard_map/all_gather | solution.py:80
  90.0 37.1 %all-reduce.9 = (bf16[2304]{0:T(1024)(128)(2,1)S(1)}, bf16[3072]{0:T(1024)(128)(2,1)S(1)}) all-reduce(bf16[2304]{0:T(1024)(128)(2,1)S(1)} %dynamic-update-slice, bf16[3072]{0:T(1024)(128)(2,1)S(1)} %dynamic-update-slice.1), channel_id=1, replica_groups=mesh['batch'=4,'seq'=8] {'batch','seq'}, use_global_device_ids=true, to_apply=%add | all-reduce | flops 5376 | bytes 21504
  127.1 42.1 %all_gather.69 = bf16[768,128]{1,0:T(8,128)(2,1)S(1)} all-gather(bf16[24,128]{1,0:T(8,128)(2,1)} %param.27), channel_id=1, replica_groups=mesh['batch'=4,'seq'=8] {'batch','seq'}, dimensions={0}, use_global_device_ids=true | all-gather | bytes 202752 | tf_op jit(solution)/shard_map/all_gather | solution.py:83
  174.7 7.8 add_convert_fusion.1
  182.6 6.6 copy.156
  189.2 3.9 slice_bitcast_fusion
  193.7 4.9 fusion.206
  198.7 4.8 fusion.207
  205.2 3.3 pad_maximum_fusion
  208.5 3.4 fusion.164
  214.7 6.6 all-gather.6
  223.3 2.1 copy.171
  225.4 38.9 %all-gather.7 = bf16[32,24,2]{1,2,0:T(2,128)(2,1)S(1)} all-gather(bf16[1,24,2]{1,2,0:T(2,128)(2,1)S(1)} %bitcast.448), channel_id=1, replica_groups=mesh['batch'=4,'seq'=8] {'batch','seq'}, dimensions={0}, use_global_device_ids=true | all-gather | bytes 3168 | tf_op jit(solution)/shard_map/all_gather | solution.py:85
  266.2 2.2 fusion.205
  268.5 2.4 fusion.204
  271.8 8.0 all-gather.1
  279.8 4.7 copy.169
  284.5 2.5 divide_convert_fusion.4
  291.2 4.8 copy.168
  297.3 23.3 %while.64 = (s32[]{:T(128)}, f32[2,12,128,64]{3,2,1,0:T(8,128)S(1)}, f32[2,12,128]{2,1,0:T(8,128)S(1)}, s32[]{:T(128)}, bf16[8,2,12,128,64]{3,4,2,1,0:T(8,128)(2...) while((s32[]{:T(128)}, ...), condition=%wide.region_14.15_spmd.clone, body=%wide.region_13.14_spmd.clone.sunk | while | flops 998408 | bytes 3569819 | solution.py:34
  321.1 79.4 %while.63 = (s32[]{:T(128)}, f32[12,2,512,64]{2,3,0,1:T(8,128)}, f32[12,2,512]{2,0,1:T(8,128)S(1)}, bf16[12,2,512,128]{3,2,1,0:T(8,128)(2,1)}, bf16[12,2,512,128...) while((s32[]{:T(128)}, f32[12,2,512,64]{2,3,0,1:T(8,128)}, ...), condition=%wide.region_17.18_spmd.clone, body=%wide.region_15.17_spmd.clone.sunk | while | flops 307954688 | bytes 4725381 | solution.py:187
  385.1 2.1 fusion.277
  398.4 2.1 fusion.277
  400.5 3.5 convert_element_type.325
  404.1 3.8 fusion.208
  408.5 11.3 fusion.123
  419.8 8.5 all-gather.21.cloned.1.call-done
  428.3 17.4 %convert_reduce_fusion = (f32[3072]{0:T(1024)}, bf16[2,512,3072]{2,1,0:T(8,128)(2,1)S(1)}) fusion(f32[2,512,3072]{2,1,0:T(8,128)} %fusion.123, f32[3072]{0:T(1024)S(1)} %copy-done.70, bf16[2,512,768]{2,1,0:T(8,128)(2,1)} %param.33, bf16[3072,768]{1,0:T(8,128)(2,1)} %all-gather.21.cloned.1.call-done), kind=kOutput, calls=%fused_computation.133 | convolution fusion | flops 4904186880 | bytes 25190400 | tf_op jit(solution)/shard_map/rtd,fd->rtf/dot_general | solution.py:226
  445.8 6.2 multiply_reduce_fusion
  464.5 4.4 fusion.145
  469.0 9.2 all-gather.3
  478.2 2.8 convolution_bitcast_fusion.5
  481.1 12.3 %all-gather.25.cloned.1.call-done = bf16[16,12,128,64]{2,3,1,0:T(8,128)(2,1)} async-done(((bf16[2,12,128,64]{2,3,1,0:T(8,128)(2,1)}), bf16[16,12,128,64]{2,3,1,0:T(8,128)(2,1)}) %all-gather.25.cloned.1.call-update) | async-done | bytes 3145744 | tf_op jit(solution)/shard_map/all_gather | solution.py:16
  493.4 23.3 %while.65 = (s32[]{:T(128)}, f32[2,12,128,64]{3,2,1,0:T(8,128)S(1)}, f32[2,12,128]{2,1,0:T(8,128)S(1)}, s32[]{:T(128)}, bf16[8,2,12,128,64]{3,4,2,1,0:T(8,128)(2...) while((s32[]{:T(128)}, ...), condition=%wide.region_24.25_spmd.clone, body=%wide.region_23.24_spmd.clone.sunk | while | flops 998412 | bytes 3569881 | solution.py:34
  517.2 171.3 %while.66 = (s32[]{:T(128)}, f32[12,2,512,128]{2,3,1,0:T(8,128)}, f32[12,2,512,128]{2,3,1,0:T(8,128)}, bf16[12,2,512,64]{2,3,1,0:T(8,128)(2,1)}, bf16[12,2,512,6...) while((s32[]{:T(128)}, f32[12,2,512,128]{2,3,1,0:T(8,128)}, ...), condition=%wide.region_26.27_spmd.clone.clone, body=%wide.region_25.26_spmd.clone.clone.sunk | while | flops 847249408 | bytes 14026417 | solution.py:327
  529.0 2.5 fusion.306
  543.3 2.5 fusion.306
  557.5 2.5 fusion.306
  571.8 2.5 fusion.306
  586.1 2.5 fusion.306
  600.3 2.5 fusion.306
  614.5 2.5 fusion.306
  628.8 2.5 fusion.306
  643.0 2.5 fusion.306
  657.2 2.5 fusion.306
  671.5 2.5 fusion.306
  685.8 2.5 fusion.306
  688.5 6.9 multiply_reduce_fusion.4
  695.6 5.1 multiply_reduce_fusion.2
  704.7 5.0 add_convert_fusion.3
  712.4 2.3 reshape.357
  714.8 11.0 convolution_bitcast_fusion.1
  726.5 13.4 %convolution_bitcast_fusion = f32[3072,768]{1,0:T(8,128)} fusion(bf16[2,512,768]{2,1,0:T(8,128)(2,1)} %param.33, f32[2,512,3072]{2,1,0:T(8,128)} %fusion.123, f32[3072]{0:T(1024)S(1)} %copy-done.71), kind=kOutput, calls=%fused_computation.138 | convolution fusion | flops 4863295488 | bytes 23605248 | tf_op jit(solution)/shard_map/rtf,rtd->fd/dot_general | solution.py:222
  740.9 2.2 convolution_bitcast_fusion.4
  745.4 2.2 copy-done.31
  747.6 6.7 convolution_bitcast_fusion.2
  755.1 13.1 %add_convert_fusion.5 = bf16[2,512,768]{2,1,0:T(8,128)(2,1)} fusion(f32[2,512,768]{2,1,0:T(8,128)S(1)} %copy-done.10, bf16[3072,768]{1,0:T(8,128)(2,1)} %all-gather.21.cloned.1.call-done, f32[768]{0:T(1024)S(1)} %copy-done.77, f32[2,512,3072]{2,1,0:T(8,128)} %fusion.123, f32[3072]{0:T(1024)S(1)} %copy-done.71), kind=kOutput, calls=%fused_computation.202 | convolution fusion | flops 4865654784 | bytes 22035456 | tf_op jit(solution)/shard_map/rtf,fd->rtd/dot_general | solution.py:210
  768.2 4.7 fusion.198
  775.3 2.5 convert_reduce_fusion.3
  778.0 40.4 %all-reduce.8 = (f32[2,768]{1,0:T(2,128)S(1)}, f32[2,768]{1,0:T(2,128)S(1)}, f32[2304]{0:T(1024)S(1)}, f32[2,768]{1,0:T(2,128)S(1)}, f32[3072]{0:T(1024)S(1)}) all-reduce(f32[2,768]{1,0:T(2,128)S(1)} %pad_maximum_fusion.2, f32[2,768]{1,0:T(2,128)S(1)} %pad_maximum_fusion.3, ...), channel_id=6, replica_groups=mesh['batch'=4,'seq'=8] {'batch','seq'}, use_global_device_ids=true, to_apply=%region_35.36.clone | all-reduce | flops 9984 | bytes 79872
  821.5 129.6 %reduce-scatter.15.cloned.1.call-done = f32[24,3072]{1,0:T(8,128)} async-done(((f32[768,3072]{1,0:T(8,128)}), f32[24,3072]{1,0:T(8,128)}) %reduce-scatter.15.cloned.1.call-update) | async-done | bytes 294928 | tf_op jit(solution)/shard_map/reduce_scatter | solution.py:384
  951.1 141.9 %reduce-scatter.17.cloned.1.call-done = f32[96,768]{1,0:T(8,128)} async-done(((f32[3072,768]{1,0:T(8,128)}), f32[96,768]{1,0:T(8,128)}) %reduce-scatter.17.cloned.1.call-update) | async-done | bytes 294928 | tf_op jit(solution)/shard_map/reduce_scatter | solution.py:386
  1093.0 124.3 %reduce-scatter.11.cloned.1.call-done = f32[24,2304]{1,0:T(8,128)} async-done(((f32[768,2304]{1,0:T(8,128)}), f32[24,2304]{1,0:T(8,128)}) %reduce-scatter.11.cloned.1.call-update) | async-done | bytes 221200 | tf_op jit(solution)/shard_map/reduce_scatter | solution.py:379
  (632 shorter events, 314.4 us)
Async XLA Ops:
  7.2 164.6 %copy-start.81 = (s32[2,4]{1,0:T(2,128)S(1)}, s32[2,4]{1,0:T(2,128)}, u32[]{:S(2)}) copy-start(s32[2,4]{1,0:T(2,128)} %param.22) | copy-start | bytes 100
  7.2 165.9 %copy-start.12 = (bf16[2,512,768]{2,1,0:T(8,128)(2,1)S(1)}, bf16[2,512,768]{2,1,0:T(8,128)(2,1)}, u32[]{:S(2)}) copy-start(bf16[2,512,768]{2,1,0:T(8,128)(2,1)} %param.21) | copy-start | bytes 4718596
  7.2 167.5 %all-gather.15.cloned.1.call-start = ((), (), s32[]{:S(2)}) async-start(), calls=%async_computation.5 | async-start | bytes 3649536 | tf_op jit(solution)/shard_map/all_gather | solution.py:81
  7.9 289.3 %all-gather.23.cloned.1.call-start = ((), (), s32[]{:S(2)}) async-start(), calls=%async_computation.13 | async-start | bytes 3538944 | tf_op jit(solution)/shard_map/all_gather | solution.py:16
  171.2 21.9 %copy-start.35 = (bf16[12,64,1,64]{1,3,0,2:T(8,128)(2,1)}, bf16[12,64,1,64]{1,3,0,2:T(8,128)(2,1)S(1)}, u32[]{:S(2)}) copy-start(bf16[12,64,1,64]{1,3,0,2:T(8,128)(2,1)S(1)} %copy.251) | copy-start | bytes 294916
  172.9 9.7 copy-start.67
  173.1 9.5 copy-start.58
  173.1 9.5 copy-start.75
  173.4 9.2 copy-start.53
  174.0 8.6 copy-start.64
  174.1 8.6 copy-start.60
  174.7 30.5 %copy-start.73 = (bf16[2,512]{1,0:T(2,128)(2,1)}, bf16[2,512]{1,0:T(2,128)(2,1)S(1)}, u32[]{:S(2)}) copy-start(bf16[2,512]{1,0:T(2,128)(2,1)S(1)} %get-tuple-element.911) | copy-start | bytes 6148
  193.1 5.5 copy-start.16
  193.1 72.5 %copy-start.18 = (bf16[2,512,1,12,64]{1,4,3,2,0:T(8,128)(2,1)}, bf16[2,512,1,12,64]{1,4,3,2,0:T(8,128)(2,1)S(1)}, u32[]{:S(2)}) copy-start(bf16[2,512,1,12,64]{1,4,3,2,0:T(8,128)(2,1)S(1)} %get-tuple-element.920) | copy-start | bytes 4718596
  198.7 4.9 copy-start
  208.5 16.9 %copy-start.83 = (bf16[2,24]{1,0:T(2,128)(2,1)S(1)}, bf16[2,24]{1,0:T(2,128)(2,1)}, u32[]{:S(2)}) copy-start(bf16[2,24]{1,0:T(2,128)(2,1)} %param.29) | copy-start | bytes 292
  211.9 192.1 %all-gather.17.cloned.1.call-start = ((), (), s32[]{:S(2)}) async-start(), calls=%async_computation.6 | async-start | bytes 1216512 | tf_op jit(solution)/shard_map/all_gather | solution.py:84
  212.7 195.8 %all-gather.19.cloned.1.call-start = ((), (), s32[]{:S(2)}) async-start(), calls=%async_computation.7 | async-start | bytes 4866048 | tf_op jit(solution)/shard_map/all_gather | solution.py:86
  213.3 215.1 %all-gather.21.cloned.1.call-start = ((), (), s32[]{:S(2)}) async-start(), calls=%async_computation.8 | async-start | bytes 4866048 | tf_op jit(solution)/shard_map/all_gather | solution.py:88
  213.8 279.5 %all-gather.25.cloned.1.call-start = ((), (), s32[]{:S(2)}) async-start(), calls=%async_computation.14 | async-start | bytes 3538944 | tf_op jit(solution)/shard_map/all_gather | solution.py:16
  223.3 45.1 %copy-start.37 = (bf16[12,64,1,64]{1,3,0,2:T(8,128)(2,1)}, bf16[12,64,1,64]{1,3,0,2:T(8,128)(2,1)S(1)}, u32[]{:S(2)}) copy-start(bf16[12,64,1,64]{1,3,0,2:T(8,128)(2,1)S(1)} %copy.249) | copy-start | bytes 294916
  291.2 4.8 copy-start.20
  297.3 23.8 %copy-start.46 = (f32[12,2,512]{2,0,1:T(8,128)S(1)}, f32[12,2,512]{2,0,1:T(8,128)}, u32[]{:S(2)}) copy-start(f32[12,2,512]{2,0,1:T(8,128)} %custom-call.5) | copy-start | bytes 147460
  297.3 23.8 %copy-start.47 = (pred[512,512]{0,1:T(8,128)(4,1)S(1)}, pred[512,512]{0,1:T(8,128)(4,1)}, u32[]{:S(2)}) copy-start(pred[512,512]{0,1:T(8,128)(4,1)} %copy.171) | copy-start | bytes 786436
  297.3 23.8 %copy-start.68 = (s32[2,512]{1,0:T(2,128)S(1)}, s32[2,512]{1,0:T(2,128)}, u32[]{:S(2)}) copy-start(s32[2,512]{1,0:T(2,128)} %copy-done.67) | copy-start | bytes 12292
  400.5 3.6 copy-start.39
  400.5 7.4 copy-start.57
  400.5 3.6 copy-start.78
  407.9 44.0 %copy-start.9 = (f32[2,512,768]{2,1,0:T(8,128)}, f32[2,512,768]{2,1,0:T(8,128)S(1)}, u32[]{:S(2)}) copy-start(f32[2,512,768]{2,1,0:T(8,128)S(1)} %get-tuple-element.942) | copy-start | bytes 9437188
  408.0 44.0 %copy-start.51 = (f32[2,512]{1,0:T(2,128)}, f32[2,512]{1,0:T(2,128)S(1)}, u32[]{:S(2)}) copy-start(f32[2,512]{1,0:T(2,128)S(1)} %broadcast_multiply_fusion.2) | copy-start | bytes 12292
  408.5 43.5 %copy-start.55 = (f32[2,512]{1,0:T(2,128)}, f32[2,512]{1,0:T(2,128)S(1)}, u32[]{:S(2)}) copy-start(f32[2,512]{1,0:T(2,128)S(1)} %fusion.193) | copy-start | bytes 12292
  408.5 19.8 %copy-start.70 = (f32[3072]{0:T(1024)S(1)}, f32[3072]{0:T(1024)}, u32[]{:S(2)}) copy-start(f32[3072]{0:T(1024)} %convert_element_type.335) | copy-start | bytes 36868
  428.3 17.4 %copy-start.84 = (bf16[768,3072]{1,0:T(8,128)(2,1)S(1)}, bf16[768,3072]{1,0:T(8,128)(2,1)}, u32[]{:S(2)}) copy-start(bf16[768,3072]{1,0:T(8,128)(2,1)} %all-gather.19.cloned.1.call-done) | copy-start | bytes 14155780
  445.8 6.2 copy-start.24
  461.8 16.4 %copy-start.40 = (bf16[12,2,512,64]{2,3,0,1:T(8,128)(2,1)S(1)}, bf16[12,2,512,64]{2,3,0,1:T(8,128)(2,1)}, u32[]{:S(2)}) copy-start(bf16[12,2,512,64]{2,3,0,1:T(8,128)(2,1)} %convert_element_type.325) | copy-start | bytes 4718596
  461.8 359.7 %reduce-scatter.13.cloned.1.call-start = ((), (), s32[]{:S(2)}) async-start(), calls=%async_computation.10 | async-start | bytes 2433024 | tf_op jit(solution)/shard_map/reduce_scatter | solution.py:382
  461.9 16.3 %copy-start.42 = (bf16[2,512,768]{2,1,0:T(8,128)(2,1)S(1)}, bf16[2,512,768]{2,1,0:T(8,128)(2,1)}, u32[]{:S(2)}) copy-start(bf16[2,512,768]{2,1,0:T(8,128)(2,1)} %copy-done.41) | copy-start | bytes 4718596
  481.0 340.5 %reduce-scatter.19.cloned.1.call-start = ((), (), s32[]{:S(2)}) async-start(), calls=%async_computation.15 | async-start | bytes 405504
  493.4 23.8 %copy-start.44 = (pred[512,512]{1,0:T(8,128)(4,1)S(1)}, pred[512,512]{1,0:T(8,128)(4,1)}, u32[]{:S(2)}) copy-start(pred[512,512]{1,0:T(8,128)(4,1)} %iota_compare_fusion) | copy-start | bytes 786436
  493.4 23.8 %copy-start.69 = (s32[2,512]{1,0:T(2,128)S(1)}, s32[2,512]{1,0:T(2,128)}, u32[]{:S(2)}) copy-start(s32[2,512]{1,0:T(2,128)} %copy-done.67) | copy-start | bytes 12292
  517.2 171.3 %copy-start.49 = (f32[2,512,12]{1,0,2:T(2,128)S(1)}, f32[2,512,12]{1,0,2:T(2,128)}, u32[]{:S(2)}) copy-start(f32[2,512,12]{1,0,2:T(2,128)} %multiply_divide_fusion.2) | copy-start | bytes 147460
  517.2 171.3 %copy-start.50 = (f32[2,512,12]{1,0,2:T(2,128)S(1)}, f32[2,512,12]{1,0,2:T(2,128)}, u32[]{:S(2)}) copy-start(f32[2,512,12]{1,0,2:T(2,128)} %multiply_divide_fusion.3) | copy-start | bytes 147460
  688.5 7.0 copy-start.1
  688.5 7.0 copy-start.3
  688.5 7.0 copy-start.48
  695.5 5.2 copy-start.4
  695.5 5.2 copy-start.6
  695.5 6.5 copy-start.11
  704.1 5.5 copy-start.21
  704.6 5.0 copy-start.17
  710.8 4.0 copy-start.10
  710.8 4.0 copy-start.52
  710.8 4.0 copy-start.56
  714.7 236.3 %reduce-scatter.15.cloned.1.call-start = ((), (), s32[]{:S(2)}) async-start(), calls=%async_computation.11 | async-start | bytes 9732096 | tf_op jit(solution)/shard_map/reduce_scatter | solution.py:384
  725.8 367.2 %reduce-scatter.17.cloned.1.call-start = ((), (), s32[]{:S(2)}) async-start(), calls=%async_computation.12 | async-start | bytes 9732096 | tf_op jit(solution)/shard_map/reduce_scatter | solution.py:386
  740.0 3.1 copy-start.36
  740.0 477.3 %reduce-scatter.11.cloned.1.call-start = ((), (), s32[]{:S(2)}) async-start(), calls=%async_computation.9 | async-start | bytes 7299072 | tf_op jit(solution)/shard_map/reduce_scatter | solution.py:379
  744.7 2.9 copy-start.13
  744.7 2.9 copy-start.54
  744.7 2.9 copy-start.59
  755.1 13.1 %copy-start.14 = (bf16[2,512,768]{2,1,0:T(8,128)(2,1)S(1)}, bf16[2,512,768]{2,1,0:T(8,128)(2,1)}, u32[]{:S(2)}) copy-start(bf16[2,512,768]{2,1,0:T(8,128)(2,1)} %param.21) | copy-start | bytes 4718596
  755.1 13.1 %copy-start.32 = (bf16[2,512,3,12,64]{1,4,3,2,0:T(8,128)(2,1)S(1)}, bf16[2,512,3,12,64]{1,4,3,2,0:T(8,128)(2,1)}, u32[]{:S(2)}) copy-start(bf16[2,512,3,12,64]{1,4,3,2,0:T(8,128)(2,1)} %copy-done.31) | copy-start | bytes 14155780
  755.1 13.1 %copy-start.85 = (bf16[768,2304]{1,0:T(8,128)(2,1)S(1)}, bf16[768,2304]{1,0:T(8,128)(2,1)}, u32[]{:S(2)}) copy-start(bf16[768,2304]{1,0:T(8,128)(2,1)} %all-gather.15.cloned.1.call-done) | copy-start | bytes 10616836
  768.2 4.8 copy-start.65
  (34 other events, 61.7 us)
Sparse Core Ops, SparseCore 0:
  10.9 62.7 all-gather.14
  212.1 28.4 all-gather.22
  243.5 54.0 all-gather.16
  300.3 62.7 all-gather.18
  365.8 62.4 all-gather.20
  461.9 31.3 all-gather.24
  499.2 99.1 reduce-scatter.12
  714.8 94.8 reduce-scatter.18
  816.2 134.7 reduce-scatter.14
  958.4 134.5 reduce-scatter.16
  1099.3 117.9 reduce-scatter.10
where the time goes:
time: 1240 us; the launch traced here: 1220 us
  waiting for transfers between devices  419 us (34%)
  matrix products  329 us (27%)
  blocking collectives  262 us (21%)
  local copies, waits for them, and re-layouts  109 us (9%)
  other arithmetic  86.2 us (7%)
  between operations  16.1 us (1%)
    reduce_scatter x1, waiting for transfers between devices, local(): lax.psum_scatter(shrink_grad_sum, ('batch', 'seq'), scatter_dimension=0,...  142 us
    reduce_scatter x1, waiting for transfers between devices, local(): lax.psum_scatter(expand_grad_sum, ('batch', 'seq'), scatter_dimension=0,...  130 us
    reduce_scatter x1, waiting for transfers between devices, local(): lax.psum_scatter(mixing_grad_sum, ('batch', 'seq'), scatter_dimension=0,...  124 us
    unnamed x2, blocking collectives  77.5 us
    all_gather x1, blocking collectives, local(): lax.all_gather(norm_gains, ('batch', 'seq'), axis=1, tiled=True)  43.3 us
    all_gather x1, blocking collectives, local(): lax.all_gather(feature_maps, ('batch', 'seq'), axis=0, tiled=True)  42.1 us
    all_gather x1, blocking collectives, local(): lax.all_gather(branch_offsets, ('batch', 'seq'), axis=1, tiled=True)  38.9 us
    all_gather x1, blocking collectives, local(): lax.all_gather(norm_shifts, ('batch', 'seq'), axis=1, tiled=True)  36.8 us
  transfers between devices with their start and end apart: 11, of which 5 were waited for; matrix products, arithmetic and copies ran while one was open for 36% of the time, Pallas kernels for 0%

commit v1 on v0

v1 whole, which is shorter than its diff:
```python
import functools

import jax
import jax.numpy as jnp
from jax import lax
from jax.experimental import pallas as pl
from jax.experimental.pallas import tpu as pltpu
from jax.sharding import PartitionSpec as P

HD = 64
F = 2 * HD
PAIR = 2 * HD
SUB = 256
WIRE = F + 16
EPSILON = 1e-05
AXES = ("batch", "seq")
VMEM = 56 * 1024 * 1024
bf16 = jnp.bfloat16
f32 = jnp.float32


def dot(a, b, left, right):
    return lax.dot_general(a, b, (((left,), (right,)), ((), ())), preferred_element_type=f32)


def nn(a, b):
    return dot(a, b, 1, 0)


def nt(a, b):
    return dot(a, b, 1, 1)


def tn(a, b):
    return dot(a, b, 0, 0)


def lane(shape):
    return lax.broadcasted_iota(jnp.int32, shape, len(shape) - 1)


def sublane(shape):
    return lax.broadcasted_iota(jnp.int32, shape, len(shape) - 2)


def normalize(values):
    center = jnp.mean(values, axis=-1, keepdims=True)
    centered = values - center
    spread = jnp.mean(centered * centered, axis=-1, keepdims=True)
    scale = lax.rsqrt(spread + EPSILON)
    return centered * scale, scale


def normalize_back(upstream, xhat, scale, gain):
    entry = upstream * gain
    first = jnp.mean(entry, axis=-1, keepdims=True)
    second = jnp.mean(entry * xhat, axis=-1, keepdims=True)
    return scale * (entry - first - xhat * second)


def map_weight(rows, keys):
    rows = rows.astype(f32)
    turned = pltpu.roll(rows, HD, 1)
    low = lane(rows.shape) < HD
    signed = jnp.where(low, turned, -rows) if keys else jnp.where(low, rows, -turned)
    top = sublane(rows.shape) < HD
    return jnp.concatenate(
        [jnp.where(top, signed, 0.0), jnp.where(top, 0.0, signed)], axis=1
    ).astype(bf16)


def segment_ones(width):
    shape = (width, width)
    return (lane(shape) // HD == sublane(shape) // HD).astype(bf16)


def segment_sum(values, ones):
    high = values.astype(bf16)
    low = (values - high.astype(f32)).astype(bf16)
    return nn(high, ones) + nn(low, ones)


def features(logits, ones):
    parts = []
    for at in range(0, logits.shape[1], F):
        part = logits[:, at : at + F]
        low = lane(part.shape) < HD
        first = jnp.max(jnp.where(low, part, -jnp.inf), axis=1, keepdims=True)
        second = jnp.max(jnp.where(low, -jnp.inf, part), axis=1, keepdims=True)
        parts.append(jnp.exp(part - jnp.where(low, first, second)))
    powers = jnp.concatenate(parts, axis=1)
    return powers / nn(powers.astype(bf16), ones)


def features_back(phi, upstream, ones):
    phi = phi.astype(f32)
    return phi * (upstream - segment_sum(phi * upstream, ones))


def with_aux(pair, head, aux):
    own = (lane(pair.shape) < HD) if head == 0 else (lane(pair.shape) >= HD)
    return jnp.where(own, pair, aux)


def pair_rows(first, second):
    top = sublane(first.shape) < HD
    return jnp.where(top, first, second)


def put_wire(ref, at, first, second, aux_rows):
    ref[0, at, 0:F, :] = pair_rows(first, second).astype(bf16)
    sums = [sum(x[a : a + 1] for a in rows) for x, rows in zip((first, second), aux_rows)]
    row = sublane((16, F))
    ref[0, at, F:WIRE, :] = jnp.where(
        row == 0, sums[0], jnp.where(row == 1, sums[1], 0.0)
    ).astype(bf16)


def take_wire(ref, at):
    state = ref[0, at, 0:F, :]
    sums = ref[0, at, F:WIRE, :]
    top = sublane(state.shape) < HD
    return jnp.where(top, state, sums[0:1]), jnp.where(top, sums[1:2], state)


def block_masks(split, count, flipped):
    masks = {}
    for ib in range(count):
        for jb in range(ib + 1):
            shape = (SUB, SUB)
            i = (lane(shape) if flipped else sublane(shape)) + ib * SUB
            j = (sublane(shape) if flipped else lane(shape)) + jb * SUB
            mask = (i < split) | (j >= split)
            if ib == jb:
                mask = mask & (j <= i)
            masks[ib, jb] = mask
    return masks


def keys_kernel(
    split_ref, tok, gain, shift, wk, wv, ok, ov, maps, normed_o, k_o, v_o, phi_o, wire_o, kept
):
    row, quad = pl.program_id(0), pl.program_id(1)

    @pl.when(quad == 0)
    def _():
        xhat, _ = normalize(tok[...].astype(f32))
        normed = (xhat * gain[...] + shift[...]).astype(bf16)
        kept[...] = normed
        normed_o[...] = normed

    normed = kept[...]
    keys = (nn(normed, wk[...]) + ok[...]).astype(bf16)
    values = (nn(normed, wv[...]) + ov[...]).astype(bf16)
    k_o[...] = keys
    v_o[...] = values
    count = keys.shape[0]
    split = split_ref[row]
    begin = jnp.where(split < count, split, 0)
    last = sublane((count, PAIR)) >= begin
    ones = segment_ones(2 * F)
    for p in range(2):
        at = slice(p * PAIR, (p + 1) * PAIR)
        phi = features(nn(keys[:, at], map_weight(maps[at, :], True)), ones).astype(bf16)
        phi_o[:, 2 * p * F : 2 * (p + 1) * F] = phi
        pair = values[:, at].astype(f32)
        sums = [
            tn(
                jnp.where(last, with_aux(pair, h, 1.0), 0.0).astype(bf16),
                phi[:, h * F : (h + 1) * F],
            )
            for h in range(2)
        ]
        put_wire(wire_o, p, sums[0], sums[1], ((HD,), (0,)))


def local_kernel(split_ref, normed, wq, oq, maps, phi_key, val, q_o, phi_o, num_o):
    row = pl.program_id(0)
    queries = (nn(normed[...], wq[...]) + oq[...]).astype(bf16)
    q_o[...] = queries
    count = queries.shape[0]
    split = split_ref[row]
    blocks = count // SUB
    masks = block_masks(split, blocks, False)
    ones = segment_ones(2 * F)
    for p in range(2):
        at = slice(p * PAIR, (p + 1) * PAIR)
        phi = features(nn(queries[:, at], map_weight(maps[at, :], False)), ones).astype(bf16)
        phi_o[:, 2 * p * F : 2 * (p + 1) * F] = phi
        pair = val[:, at].astype(f32)
        for h in range(2):
            column = slice((2 * p + h) * F, (2 * p + h + 1) * F)
            query = phi[:, h * F : (h + 1) * F]
            key = phi_key[:, column]
            extended = with_aux(pair, h, 1.0).astype(bf16)
            for ib in range(blocks):
                rows = slice(ib * SUB, (ib + 1) * SUB)
                total = None
                for jb in range(ib + 1):
                    others = slice(jb * SUB, (jb + 1) * SUB)
                    scores = nt(query[rows], key[others])
                    scores = jnp.where(masks[ib, jb], scores, 0.0).astype(bf16)
                    part = nn(scores, extended[others])
                    total = part if total is None else total + part
                num_o[rows, column] = total


def middle_kernel(
    split_ref, num, phi_query, wire, tok, wo, bias, gain, shift, att_o, rden_o, mid_o, normed_o
):
    row = pl.program_id(0)
    count = num.shape[0]
    carry = sublane((count, F)) < split_ref[row]
    for p in range(wire.shape[1]):
        sums = []
        for h, memory in enumerate(take_wire(wire, p)):
            column = slice((2 * p + h) * F, (2 * p + h + 1) * F)
            sums.append(
                num[:, column] + jnp.where(carry, nt(phi_query[:, column], memory), 0.0)
            )
        low = lane((count, PAIR)) < HD
        numerator = jnp.where(low, sums[0], sums[1])
        denominator = pltpu.roll(jnp.where(low, sums[1], sums[0]), HD, 1)
        inverse = 1.0 / denominator
        at = slice(p * PAIR, (p + 1) * PAIR)
        rden_o[:, at] = inverse
        att_o[:, at] = (numerator * inverse).astype(bf16)
    middle = tok[...].astype(f32) + nn(att_o[...], wo[...]) + bias[...]
    mid_o[...] = middle
    xhat, _ = normalize(middle)
    normed_o[...] = (xhat * gain[...] + shift[...]).astype(bf16)


def mlp_kernel(normed, cot, ex, sh, bias, y_o, back_o, eg_o, sg_o, bg_o, turned):
    step = pl.program_id(0)

    @pl.when(step == 0)
    def _():
        turned[...] = normed[...].T
        y_o[...] = jnp.zeros_like(y_o)
        back_o[...] = jnp.zeros_like(back_o)

    slope = 0.7978845608028654
    cubic = 0.044715
    pre = nn(normed[...], ex[...]) + bias[...]
    square = pre * pre
    bend = jnp.tanh(slope * (pre + cubic * pre * square))
    hidden = (0.5 * pre * (1.0 + bend)).astype(bf16)
    rise = 0.5 * (1.0 + bend) + 0.5 * pre * (1.0 - bend * bend) * slope * (
        1.0 + 3.0 * cubic * square
    )
    back = (nt(cot[...], sh[...]) * rise).astype(bf16)
    bg_o[...] = jnp.sum(back.astype(f32), axis=0, keepdims=True)
    y_o[...] += nn(hidden, sh[...])
    back_o[...] += nt(back, ex[...])
    sg_o[...] = tn(hidden, cot[...])
    eg_o[...] = nn(turned[...], back)


def column_sum(values):
    return jnp.sum(values, axis=0, keepdims=True)


def middle_back_kernel(
    split_ref,
    mid,
    y,
    back,
    cot,
    att,
    rden,
    phi_query,
    wo,
    gain,
    bias,
    out_o,
    mb_o,
    ext_o,
    wire_o,
    og_o,
    small_o,
):
    row = pl.program_id(0)

    @pl.when(row == 0)
    def _():
        og_o[...] = jnp.zeros_like(og_o)
        small_o[...] = jnp.zeros_like(small_o)

    middle = mid[...]
    upstream = cot[...].astype(f32)
    out_o[...] = (middle + y[...] + bias[...]).astype(bf16)
    xhat, scale = normalize(middle)
    from_norm = back[...]
    middle_back = upstream + normalize_back(from_norm, xhat, scale, gain[...])
    mb_o[...] = middle_back
    branch_back = middle_back.astype(bf16)
    small_o[0:1, :] += column_sum(from_norm * xhat)
    small_o[1:2, :] += column_sum(from_norm)
    small_o[2:3, :] += column_sum(branch_back.astype(f32))
    small_o[3:4, :] += column_sum(upstream)
    og_o[...] += tn(att[...], branch_back)
    attended_back = nt(branch_back, wo[...])
    count = middle.shape[0]
    carry = sublane((count, F)) < split_ref[row]
    ones = segment_ones(PAIR)
    spot = lane((count, PAIR))
    for p in range(wire_o.shape[1]):
        at = slice(p * PAIR, (p + 1) * PAIR)
        given = attended_back[:, at]
        inverse = rden[:, at]
        numerator_back = given * inverse
        denominator_back = -segment_sum(given * att[:, at].astype(f32), ones) * inverse
        aux = pltpu.roll(denominator_back, HD, 1)
        high = aux.astype(bf16).astype(f32)
        rest = aux - high
        sums = []
        for h in range(2):
            first = HD if h == 0 else 0
            extended = with_aux(
                numerator_back,
                h,
                jnp.where(spot == first, high, jnp.where(spot == first + 1, rest, 0.0)),
            ).astype(bf16)
            column = slice((2 * p + h) * F, (2 * p + h + 1) * F)
            ext_o[:, column] = extended
            query = jnp.where(carry, phi_query[:, column].astype(f32), 0.0).astype(bf16)
            sums.append(tn(extended, query))
        put_wire(wire_o, p, sums[0], sums[1], ((HD, HD + 1), (0, 1)))


def map_gradient(pair, logits_back):
    both = tn(pair, logits_back)
    rows = pair_rows(both[:, :F], both[:, F:])
    return rows - pltpu.roll(rows, HD, 1)


def local_back_kernel(
    split_ref, phi_query, phi_key, val, ext, wire, queries, maps, pq_o, mg_o, kg_o, vg_o
):
    row = pl.program_id(1)
    count = val.shape[0]
    split = split_ref[row]
    blocks = count // SUB
    masks = block_masks(split, blocks, False)
    flipped = block_masks(split, blocks, True)
    carry = sublane((count, F)) < split
    ones = segment_ones(2 * F)
    pair = val[...].astype(f32)
    memories = take_wire(wire, 0)
    grads, tops = [], []
    for h in range(2):
        column = slice(h * F, (h + 1) * F)
        query, key, given = phi_query[:, column], phi_key[:, column], ext[:, column]
        extended = with_aux(pair, h, 1.0).astype(bf16)
        query_grad = [None] * blocks
        key_grad = [None] * blocks
        value_grad = [None] * blocks

        def add(into, at, part):
            into[at] = part if into[at] is None else into[at] + part

        for ib in range(blocks):
            rows = slice(ib * SUB, (ib + 1) * SUB)
            for jb in range(ib + 1):
                others = slice(jb * SUB, (jb + 1) * SUB)
                turned = jnp.where(flipped[ib, jb], nt(key[others], query[rows]), 0.0)
                add(value_grad, jb, nn(turned.astype(bf16), given[rows]))
                turned = jnp.where(flipped[ib, jb], nt(extended[others], given[rows]), 0.0)
                add(key_grad, jb, nn(turned.astype(bf16), query[rows]))
                straight = jnp.where(masks[ib, jb], nt(given[rows], extended[others]), 0.0)
                add(query_grad, ib, nn(straight.astype(bf16), key[others]))
        kg_o[:, column] = jnp.concatenate(key_grad, axis=0)
        tops.append(jnp.concatenate(value_grad, axis=0))
        grads.append(
            jnp.concatenate(query_grad, axis=0)
            + jnp.where(carry, nn(given, memories[h]), 0.0)
        )
    vg_o[...] = jnp.where(lane(pair.shape) < HD, tops[0], tops[1])
    logits_back = features_back(phi_query[...], jnp.concatenate(grads, axis=1), ones).astype(bf16)
    pq_o[...] = nt(logits_back, map_weight(maps[...], False)).astype(bf16)
    gradient = map_gradient(queries[...], logits_back)

    @pl.when(row == 0)
    def _():
        mg_o[...] = gradient

    @pl.when(row > 0)
    def _():
        mg_o[...] += gradient


def keys_back_kernel(
    split_ref, kg, vg, phi_key, val, wire, keys, maps, from_queries, pk_o, pv_o, mg_o
):
    row = pl.program_id(1)
    count = val.shape[0]
    split = split_ref[row]
    begin = jnp.where(split < count, split, 0)
    last = sublane((count, F)) >= begin
    ones = segment_ones(2 * F)
    pair = val[...].astype(f32)
    state = wire[0, 0, 0:F, :]
    spot = sublane(state.shape)
    grads, tops = [], []
    for h, memory in enumerate(take_wire(wire, 0)):
        column = slice(h * F, (h + 1) * F)
        first = HD if h == 0 else 0
        own = (spot < HD) if h == 0 else (spot >= HD)
        memory = jnp.where(own | (spot == first), memory.astype(f32), 0.0).astype(bf16)
        extended = with_aux(pair, h, 1.0).astype(bf16)
        grads.append(kg[:, column] + jnp.where(last, nn(extended, memory), 0.0))
        tops.append(nt(phi_key[:, column], state))
    low = lane(pair.shape) < HD
    pv_o[...] = (vg[...] + jnp.where(last, jnp.where(low, tops[0], tops[1]), 0.0)).astype(bf16)
    logits_back = features_back(phi_key[...], jnp.concatenate(grads, axis=1), ones).astype(bf16)
    pk_o[...] = nt(logits_back, map_weight(maps[...], True)).astype(bf16)
    gradient = pltpu.roll(map_gradient(keys[...], logits_back), HD, 1)

    @pl.when(row == 0)
    def _():
        mg_o[...] = jnp.where(lane(gradient.shape) < HD, from_queries[...], gradient)

    @pl.when(row > 0)
    def _():
        mg_o[...] += jnp.where(lane(gradient.shape) < HD, 0.0, gradient)


def weight_back_kernel(normed, pb, wg_o, bg_o, turned):
    @pl.when(pl.program_id(0) == 0)
    def _():
        turned[...] = normed[...].T

    wg_o[...] = nn(turned[...], pb[...])
    bg_o[...] = column_sum(pb[...].astype(f32))


def input_back_kernel(pq, pk, pv, wq, wk, wv, tok, mb, gain, out_o, small_o):
    @pl.when(pl.program_id(0) == 0)
    def _():
        small_o[...] = jnp.zeros_like(small_o)

    from_norm = nt(pq[...], wq[...]) + nt(pk[...], wk[...]) + nt(pv[...], wv[...])
    xhat, scale = normalize(tok[...].astype(f32))
    small_o[0:1, :] += column_sum(from_norm * xhat)
    small_o[1:2, :] += column_sum(from_norm)
    out_o[...] = (mb[...] + normalize_back(from_norm, xhat, scale, gain[...])).astype(bf16)


def spec(shape, index):
    return pl.BlockSpec(shape, index)


def call(kernel, grid, ins, outs, scratch=(), scalars=0, name=None):
    arrays = [entry[0] for entry in ins[scalars:]]
    fetched = [entry[0] for entry in ins[:scalars]]
    return pl.pallas_call(
        kernel,
        out_shape=[jax.ShapeDtypeStruct(shape, kind) for shape, kind, _, _ in outs],
        grid_spec=pltpu.PrefetchScalarGridSpec(
            num_scalar_prefetch=scalars,
            grid=grid,
            in_specs=[spec(block, index) for _, block, index in ins[scalars:]],
            out_specs=[spec(block, index) for _, _, block, index in outs],
            scratch_shapes=list(scratch),
        ),
        compiler_params=pltpu.CompilerParams(vmem_limit_bytes=VMEM),
        name=name,
    )(*fetched, *arrays)


def gather_rows(part):
    return lax.all_gather(part, AXES, axis=0, tiled=True)


def scatter_rows(whole):
    return lax.psum_scatter(whole, AXES, scatter_dimension=0, tiled=True)


def any_start(starts, low, high):
    return jnp.any((starts >= low) & (starts <= high), axis=1)


def carried(wire, starts, tok_count, reverse):
    size, mine = lax.axis_size("seq"), lax.axis_index("seq")
    total, reached = wire, jnp.zeros_like(wire)
    span = 1
    while span < size:
        other = lax.ppermute(total, "seq", [(i, i ^ span) for i in range(size)])
        group = mine // span
        upper = group % 2 == 1
        begin = group * span
        if reverse:
            receives = jnp.logical_not(upper)
            closed = any_start(starts, (mine + 1) * tok_count, (begin + span) * tok_count - 1)
            own_closed = any_start(starts, begin * tok_count, (begin + span) * tok_count - 1)
            other_begin = (begin - span) * tok_count
            other_closed = any_start(starts, other_begin, begin * tok_count - 1)
        else:
            receives = upper
            closed = any_start(starts, begin * tok_count, mine * tok_count - 1)
            own_closed = any_start(starts, begin * tok_count, (begin + span) * tok_count - 1)
            other_begin = (begin + span) * tok_count
            other_closed = any_start(starts, other_begin, other_begin + span * tok_count - 1)
        open_here = (receives & jnp.logical_not(closed))[:, None, None, None]
        reached = reached + jnp.where(open_here, other, 0)
        own_on = jnp.where(receives, True, jnp.logical_not(other_closed))[:, None, None, None]
        other_on = jnp.where(receives, jnp.logical_not(own_closed), True)[:, None, None, None]
        total = jnp.where(own_on, total, 0) + jnp.where(other_on, other, 0)
        span *= 2
    return reached


def local(
    tokens,
    sequence_lengths,
    norm_gains,
    norm_shifts,
    mixing_weight,
    mixing_offset,
    feature_maps,
    output_weight,
    branch_offsets,
    expand_weight,
    hidden_offset,
    shrink_weight,
    cotangent,
):
    row_count, tok_count, width = tokens.shape
    count = row_count * tok_count
    heads = width // HD
    pairs, quads = heads // 2, heads // 4
    quad = 2 * PAIR
    hidden_width = expand_weight.shape[1]

    gains = lax.all_gather(norm_gains, AXES, axis=1, tiled=True).astype(f32)
    shifts = lax.all_gather(norm_shifts, AXES, axis=1, tiled=True).astype(f32)
    branches = lax.all_gather(branch_offsets, AXES, axis=1, tiled=True).astype(f32)
    offset = gather_rows(mixing_offset).astype(f32)[None]
    hidden_bias = gather_rows(hidden_offset).astype(f32)[None]
    maps = gather_rows(feature_maps)
    mixing = gather_rows(mixing_weight)
    out_weight = gather_rows(output_weight)
    expand = gather_rows(expand_weight)
    shrink = gather_rows(shrink_weight)

    place = lax.axis_index("seq") * tok_count
    starts = jnp.cumsum(sequence_lengths, axis=1) - sequence_lengths
    inside = (starts >= place) & (starts < place + tok_count)
    split = jnp.min(jnp.where(inside, starts - place, tok_count), axis=1).astype(jnp.int32)

    tok = tokens.reshape(count, width)
    cot = cotangent.reshape(count, width)
    full = lambda r, q, s: (0, 0)
    rows_ = lambda r, q, s: (r, 0)
    both = lambda r, q, s: (r, q)

    def columns(first):
        return lambda r, q, s: (0, first + q)

    normed, keys, values, phi_key, wire = call(
        keys_kernel,
        (row_count, quads),
        [
            (split, None, None),
            (tok, (tok_count, width), rows_),
            (gains[0:1], (1, width), full),
            (shifts[0:1], (1, width), full),
            (mixing, (width, quad), columns(quads)),
            (mixing, (width, quad), columns(2 * quads)),
            (offset, (1, quad), columns(quads)),
            (offset, (1, quad), columns(2 * quads)),
            (maps, (quad, F), lambda r, q, s: (q, 0)),
        ],
        [
            ((count, width), bf16, (tok_count, width), rows_),
            ((count, width), bf16, (tok_count, quad), both),
            ((count, width), bf16, (tok_count, quad), both),
            ((count, heads * F), bf16, (tok_count, 4 * F), both),
            ((row_count, pairs, WIRE, F), bf16, (1, 2, WIRE, F), lambda r, q, s: (r, q, 0, 0)),
        ],
        [pltpu.VMEM((tok_count, width), bf16)],
        1,
        "keys",
    )
    memory = carried(wire, starts, tok_count, False)
    queries, phi_query, numerator = call(
        local_kernel,
        (row_count, quads),
        [
            (split, None, None),
            (normed, (tok_count, width), rows_),
            (mixing, (width, quad), columns(0)),
            (offset, (1, quad), columns(0)),
            (maps, (quad, F), lambda r, q, s: (q, 0)),
            (phi_key, (tok_count, 4 * F), both),
            (values, (tok_count, quad), both),
        ],
        [
            ((count, width), bf16, (tok_count, quad), both),
            ((count, heads * F), bf16, (tok_count, 4 * F), both),
            ((count, heads * F), f32, (tok_count, 4 * F), both),
        ],
        [],
        1,
        "local_attention",
    )
    one = lambda r, s: (r, 0)
    whole = lambda r, s: (0, 0)
    attended, inverse, middle, normed_mid = call(
        middle_kernel,
        (row_count,),
        [
            (split, None, None),
            (numerator, (tok_count, heads * F), one),
            (phi_query, (tok_count, heads * F), one),
            (memory, (1, pairs, WIRE, F), lambda r, s: (r, 0, 0, 0)),
            (tok, (tok_count, width), one),
            (out_weight, (width, width), whole),
            (branches[0:1], (1, width), whole),
            (gains[1:2], (1, width), whole),
            (shifts[1:2], (1, width), whole),
        ],
        [
            ((count, width), bf16, (tok_count, width), one),
            ((count, width), f32, (tok_count, width), one),
            ((count, width), f32, (tok_count, width), one),
            ((count, width), bf16, (tok_count, width), one),
        ],
        [],
        1,
        "middle",
    )
    tile = 512
    y, normed_mid_back, expand_grad, shrink_grad, hidden_grad = call(
        mlp_kernel,
        (hidden_width // tile,),
        [
            (normed_mid, (count, width), lambda f: (0, 0)),
            (cot, (count, width), lambda f: (0, 0)),
            (expand, (width, tile), lambda f: (0, f)),
            (shrink, (tile, width), lambda f: (f, 0)),
            (hidden_bias, (1, tile), lambda f: (0, f)),
        ],
        [
            ((count, width), f32, (count, width), lambda f: (0, 0)),
            ((count, width), f32, (count, width), lambda f: (0, 0)),
            ((width, hidden_width), f32, (width, tile), lambda f: (0, f)),
            ((hidden_width, width), f32, (tile, width), lambda f: (f, 0)),
            ((1, hidden_width), f32, (1, tile), lambda f: (0, f)),
        ],
        [pltpu.VMEM((width, count), bf16)],
        0,
        "mlp",
    )
    layer_output, middle_back, extended, wire_back, output_grad, small_mid = call(
        middle_back_kernel,
        (row_count,),
        [
            (split, None, None),
            (middle, (tok_count, width), one),
            (y, (tok_count, width), one),
            (normed_mid_back, (tok_count, width), one),
            (cot, (tok_count, width), one),
            (attended, (tok_count, width), one),
            (inverse, (tok_count, width), one),
            (phi_query, (tok_count, heads * F), one),
            (out_weight, (width, width), whole),
            (gains[1:2], (1, width), whole),
            (branches[1:2], (1, width), whole),
        ],
        [
            ((count, width), bf16, (tok_count, width), one),
            ((count, width), f32, (tok_count, width), one),
            ((count, heads * F), bf16, (tok_count, heads * F), one),
            ((row_count, pairs, WIRE, F), bf16, (1, pairs, WIRE, F), lambda r, s: (r, 0, 0, 0)),
            ((width, width), f32, (width, width), whole),
            ((8, width), f32, (8, width), whole),
        ],
        [],
        1,
        "middle_back",
    )
    memory_back = carried(wire_back, starts, tok_count, True)
    cell = lambda p, r, s: (r, p)
    mine = lambda p, r, s: (p, 0)
    from_wire = lambda p, r, s: (r, p, 0, 0)
    queries_back, map_query, key_feat, value_feat = call(
        local_back_kernel,
        (pairs, row_count),
        [
            (split, None, None),
            (phi_query, (tok_count, 2 * F), cell),
            (phi_key, (tok_count, 2 * F), cell),
            (values, (tok_count, PAIR), cell),
            (extended, (tok_count, 2 * F), cell),
            (memory, (1, 1, WIRE, F), from_wire),
            (queries, (tok_count, PAIR), cell),
            (maps, (PAIR, F), mine),
        ],
        [
            ((count, width), bf16, (tok_count, PAIR), cell),
            ((width, F), f32, (PAIR, F), mine),
            ((count, heads * F), f32, (tok_count, 2 * F), cell),
            ((count, width), f32, (tok_count, PAIR), cell),
        ],
        [],
        1,
        "local_back",
    )
    keys_back, values_back, map_grad = call(
        keys_back_kernel,
        (pairs, row_count),
        [
            (split, None, None),
            (key_feat, (tok_count, 2 * F), cell),
            (value_feat, (tok_count, PAIR), cell),
            (phi_key, (tok_count, 2 * F), cell),
            (values, (tok_count, PAIR), cell),
            (memory_back, (1, 1, WIRE, F), from_wire),
            (keys, (tok_count, PAIR), cell),
            (maps, (PAIR, F), mine),
            (map_query, (PAIR, F), mine),
        ],
        [
            ((count, width), bf16, (tok_count, PAIR), cell),
            ((count, width), bf16, (tok_count, PAIR), cell),
            ((width, F), f32, (PAIR, F), mine),
        ],
        [],
        1,
        "keys_back",
    )

    def weight_back(pb):
        return call(
            weight_back_kernel,
            (quads,),
            [
                (normed, (count, width), lambda q: (0, 0)),
                (pb, (count, quad), lambda q: (0, q)),
            ],
            [
                ((width, width), f32, (width, quad), lambda q: (0, q)),
                ((1, width), f32, (1, quad), lambda q: (0, q)),
            ],
            [pltpu.VMEM((width, count), bf16)],
            0,
            "weight_back",
        )

    parts = [weight_back(pb) for pb in (queries_back, keys_back, values_back)]
    mixing_grad = jnp.concatenate([p[0] for p in parts], axis=1)
    offset_grad = jnp.concatenate([p[1] for p in parts], axis=1)[0]
    row = lambda r: (r, 0)
    fixed = lambda r: (0, 0)
    input_gradient, small_in = call(
        input_back_kernel,
        (row_count,),
        [
            (queries_back, (tok_count, width), row),
            (keys_back, (tok_count, width), row),
            (values_back, (tok_count, width), row),
            (mixing, (width, width), lambda r: (0, 0)),
            (mixing, (width, width), lambda r: (0, 1)),
            (mixing, (width, width), lambda r: (0, 2)),
            (tok, (tok_count, width), row),
            (middle_back, (tok_count, width), row),
            (gains[0:1], (1, width), fixed),
        ],
        [
            ((count, width), bf16, (tok_count, width), row),
            ((8, width), f32, (8, width), fixed),
        ],
        [],
        0,
        "input_back",
    )
    gains_sum = jnp.stack([small_in[0], small_mid[0]])
    shifts_sum = jnp.stack([small_in[1], small_mid[1]])
    branch_sum = small_mid[2:4]

    def scatter_columns(rows):
        return lax.psum_scatter(rows, AXES, scatter_dimension=1, tiled=True)

    return (
        layer_output.reshape(tokens.shape),
        input_gradient.reshape(tokens.shape),
        scatter_columns(gains_sum),
        scatter_columns(shifts_sum),
        scatter_rows(mixing_grad),
        scatter_rows(offset_grad),
        scatter_rows(map_grad),
        scatter_rows(output_grad),
        scatter_columns(branch_sum),
        scatter_rows(expand_grad),
        scatter_rows(hidden_grad[0]),
        scatter_rows(shrink_grad),
    )


def solution(mesh):
    rows = P("batch", "seq", None)
    split_rows = P(AXES, None)
    split_columns = P(None, AXES)
    split_vector = P(AXES)
    return jax.shard_map(
        local,
        mesh=mesh,
        in_specs=(
            rows,
            P("batch", None),
            split_columns,
            split_columns,
            split_rows,
            split_vector,
            split_rows,
            split_rows,
            split_columns,
            split_rows,
            split_vector,
            split_rows,
            rows,
        ),
        out_specs=(
            rows,
            rows,
            split_columns,
            split_columns,
            split_rows,
            split_vector,
            split_rows,
            split_rows,
            split_columns,
            split_rows,
            split_vector,
            split_rows,
        ),
        check_vma=False,
    )
```

time: 1240 us -> 1020 us (0.82); the launches traced: 1220 us -> 1020 us
  matrix products: 329 us -> 0 us
  Pallas kernels: 0 us -> 176 us
  waiting for transfers between devices: 419 us -> 563 us
  local copies, waits for them, and re-layouts: 109 us -> 8.84 us
  other arithmetic: 86.2 us -> 12.1 us
  blocking collectives: 262 us -> 235 us
    dot_general x154 -> x0, matrix products: 329 us -> none  [the longest x12 30.2 us: head_backward(): jnp.einsum('rij,rie->rje', scores_low, numer_head, preferred_element_type...]
    pallas_call x0 -> x11, Pallas kernels: none -> 176 us  [call(): pl.pallas_call(kernel, out_shape=[jax.ShapeDtypeStruct(shape, kind) for s...]
    reduce_scatter x4, waiting for transfers between devices: 396 us -> 513 us  [scatter_rows(): return lax.psum_scatter(whole, AXES, scatter_dimension=0, tiled=True)]
    dynamic_slice x68 -> x0, local copies, waits for them, and re-layouts: 31.8 us -> none  [the longest x32 22.5 us: turn(): part[at].astype(own.dtype)]
    all_gather x7 -> x4, blocking collectives: 185 us -> 155 us  [the longest x1 40.5 us: gather_rows(): return lax.all_gather(part, AXES, axis=0, tiled=True)]
    ppermute x0 -> x6, waiting for transfers between devices: none -> 28.8 us  [carried(): other = lax.ppermute(total, 'seq', [(i, i ^ span) for i in range(size)])]
    unnamed x193 -> x23, local copies, waits for them, and re-layouts: 32.3 us -> 4.83 us
    sub x20 -> x0, other arithmetic: 25.3 us -> none  [the longest x16 10.8 us: combine(): retained = 1.0 - later[2]]
  transfers between devices with their start and end apart: 11 -> 15, of which waited for: 5 -> 9; matrix products, arithmetic and copies ran while one was open for 36% -> 2% of each run, Pallas kernels for 0% -> 10%
where the time goes in v1:
time: 1020 us
  waiting for transfers between devices  563 us (55%)
  blocking collectives  235 us (23%)
  Pallas kernels  176 us (17%)
  between operations  14.2 us (1%)
  other arithmetic  12.1 us (1%)
    reduce_scatter x4, waiting for transfers between devices, scatter_rows(): return lax.psum_scatter(whole, AXES, scatter_dimension=0, tiled=True)  513 us
    pallas_call x11, Pallas kernels, call(): pl.pallas_call(kernel, out_shape=[jax.ShapeDtypeStruct(shape, kind) for s...  176 us
    unnamed x2, blocking collectives  80 us
    all_gather x1, blocking collectives, gather_rows(): return lax.all_gather(part, AXES, axis=0, tiled=True)  40.5 us
    all_gather x1, blocking collectives, local(): gains = lax.all_gather(norm_gains, AXES, axis=1, tiled=True).astype(f32)  40.3 us
    all_gather x1, blocking collectives, local(): lax.all_gather(branch_offsets, AXES, axis=1, tiled=True).astype(f32)  38 us
    all_gather x1, blocking collectives, local(): shifts = lax.all_gather(norm_shifts, AXES, axis=1, tiled=True).astype(f32)  36.6 us
    ppermute x6, waiting for transfers between devices, carried(): other = lax.ppermute(total, 'seq', [(i, i ^ span) for i in range(size)])  28.8 us
  transfers between devices with their start and end apart: 15, of which 9 were waited for; matrix products, arithmetic and copies ran while one was open for 2% of the time, Pallas kernels for 10%

profile of v1, /device:TPU:0, one launch (start us, length us, event | category | flops | bytes accessed | tf_op | source)
XLA Modules:
  0.0 1016.5 jit_solution(5444536458683987212)
XLA Ops:
  7.2 0.7 all-gather.8.cloned.1.call-update
  8.0 0.7 all-gather.10.cloned.1.call-update
  8.7 0.7 all-gather.12.cloned.1.call-update
  9.4 0.5 all-gather.14.cloned.1.call-update
  10.1 0.9 reduce_window_sum.11
  11.0 0.8 dynamic-update-slice
  11.8 0.8 dynamic-update-slice.1
  12.6 42.2 %all-reduce.9 = (bf16[2304]{0:T(1024)(128)(2,1)S(1)}, bf16[3072]{0:T(1024)(128)(2,1)S(1)}) all-reduce(bf16[2304]{0:T(1024)(128)(2,1)S(1)} %dynamic-update-slice, bf16[3072]{0:T(1024)(128)(2,1)S(1)} %dynamic-update-slice.1), channel_id=1, replica_groups=mesh['batch'=4,'seq'=8] {'batch','seq'}, use_global_device_ids=true, to_apply=%add | all-reduce | flops 5376 | bytes 21504
  54.8 0.6 reshape.94.ok.ov.oq
  55.4 0.6 broadcast_in_dim.152
  56.0 40.3 %all-gather = bf16[32,24,2]{1,2,0:T(2,128)(2,1)S(1)} all-gather(bf16[1,24,2]{1,2,0:T(2,128)(2,1)} %bitcast.40), channel_id=1, replica_groups=mesh['batch'=4,'seq'=8] {'batch','seq'}, dimensions={0}, use_global_device_ids=true | all-gather | bytes 3168 | tf_op jit(solution)/shard_map/all_gather | solution.py:536
  96.4 0.1 copy.34
  96.5 36.6 %all-gather.1 = bf16[32,24,2]{1,2,0:T(2,128)(2,1)S(1)} all-gather(bf16[1,24,2]{1,2,0:T(2,128)(2,1)} %bitcast.41), channel_id=1, replica_groups=mesh['batch'=4,'seq'=8] {'batch','seq'}, dimensions={0}, use_global_device_ids=true | all-gather | bytes 3168 | tf_op jit(solution)/shard_map/all_gather | solution.py:537
  133.1 38.0 %all-gather.2 = bf16[32,24,2]{1,2,0:T(2,128)(2,1)S(1)} all-gather(bf16[1,24,2]{1,2,0:T(2,128)(2,1)} %bitcast.42), channel_id=1, replica_groups=mesh['batch'=4,'seq'=8] {'batch','seq'}, dimensions={0}, use_global_device_ids=true | all-gather | bytes 3168 | tf_op jit(solution)/shard_map/all_gather | solution.py:538
  171.2 0.1 reshape.108
  171.4 0.1 reshape.107
  171.6 0.1 reshape.106
  171.7 40.5 %all_gather.34.maps = bf16[768,128]{1,0:T(8,128)(2,1)} all-gather(bf16[24,128]{1,0:T(8,128)(2,1)} %param.19), channel_id=1, replica_groups=mesh['batch'=4,'seq'=8] {'batch','seq'}, dimensions={0}, use_global_device_ids=true | all-gather | bytes 202752 | tf_op jit(solution)/shard_map/all_gather | solution.py:473
  212.3 1.0 and_reduce_fusion.4
  213.2 0.6 fusion.split_ref
  213.9 0.6 fusion.4
  214.5 0.6 fusion.5
  215.1 15.6 %keys.1 = (bf16[1024,768]{1,0:T(8,128)(2,1)}, bf16[1024,768]{1,0:T(8,128)(2,1)}, bf16[1024,768]{1,0:T(8,128)(2,1)}, bf16[1024,1536]{1,0:T(8,128)(2,1)}, bf16[2,6,144,128]{3,2,1,0:T(8,128)(2,1)}) custom-call(s32[2]{0:T(128)} %fusion.split_ref, bf16[1024,768]{1,0:T(8,128)(2,1)} %bitcast.30, f32[1,768]{1,0:T(1,128)} %get-tuple-element.117.gain, ...), custom_call_target="tpu_custom_call" | custom-call | tf_op jit(solution)/shard_map/keys/pallas_call | solution.py:457
  230.6 0.4 collective-permute-start
  231.0 1.6 collective-permute-done
  232.7 1.1 select_add_fusion.5
  233.8 1.7 collective-permute-start.1
  235.6 14.7 %collective-permute-done.1 = bf16[2,6,144,128]{3,2,1,0:T(8,128)(2,1)S(1)} collective-permute-done((bf16[2,6,144,128]{3,2,1,0:T(8,128)(2,1)S(1)}, bf16[2,6,144,128]{3,2,1,0:T(8,128)(2,1)S(1)}, u32[]{:S(2)}, u32[]{:S(2)}) %collective-permute-start.1) | collective-permute-done | bytes 442400 | tf_op jit(solution)/shard_map/ppermute | solution.py:489
  250.2 0.1 select_add_fusion.4
  250.5 0.6 fusion.3
  251.1 20.8 %local_attention.1 = (bf16[1024,768]{1,0:T(8,128)(2,1)}, bf16[1024,1536]{1,0:T(8,128)(2,1)}, f32[1024,1536]{1,0:T(8,128)}) custom-call(s32[2]{0:T(128)} %fusion.split_ref, bf16[1024,768]{1,0:T(8,128)(2,1)} %get-tuple-element.50.normed, bf16[768,2304]{1,0:T(8,128)(2,1)} %all-gather.8.cloned.1.call-done.wk.wv.wq, f32[1,2304]{1,0:T(1,128)} %reshape.94.ok.ov.oq, ...), custom_call_target="tpu_custom_call" | custom-call | tf_op jit(solution)/shard_map/local_attention/pallas_call | solution.py:457
  271.9 0.9 select_add_fusion.3.wire
  272.8 9.5 middle.1
  282.3 36.7 %mlp.1 = (f32[1024,768]{1,0:T(8,128)}, f32[1024,768]{1,0:T(8,128)}, f32[768,3072]{1,0:T(8,128)}, f32[3072,768]{1,0:T(8,128)}, f32[1,3072]{1,0:T(1,128)}) custom-call(bf16[1024,768]{1,0:T(8,128)(2,1)} %get-tuple-element.57.normed, bf16[1024,768]{1,0:T(8,128)(2,1)} %bitcast.33, bf16[768,3072]{1,0:T(8,128)(2,1)} %all-gather.12.cloned.1.call-done.ex, ...), custom_call_target="tpu_custom_call" | custom-call | tf_op jit(solution)/shard_map/mlp/pallas_call | solution.py:457
  319.0 17.1 %middle_back.1 = (bf16[1024,768]{1,0:T(8,128)(2,1)}, f32[1024,768]{1,0:T(8,128)}, bf16[1024,1536]{1,0:T(8,128)(2,1)}, bf16[2,6,144,128]{3,2,1,0:T(8,128)(2,1)}, f32[768,768]{1,0:T(8,128)}, /*index=5*/f32[8,768]{1,0:T(8,128)}) custom-call(s32[2]{0:T(128)} %fusion.split_ref, f32[1024,768]{1,0:T(8,128)} %get-tuple-element.56.mid, ...), custom_call_target="tpu_custom_call" | custom-call | tf_op jit(solution)/shard_map/middle_back/pallas_call | solution.py:457
  336.2 2.0 collective-permute-done.3
  338.2 1.1 select_add_fusion.2
  339.3 2.6 collective-permute-start.4
  341.9 10.5 %collective-permute-done.4 = bf16[2,6,144,128]{3,2,1,0:T(8,128)(2,1)S(1)} collective-permute-done((bf16[2,6,144,128]{3,2,1,0:T(8,128)(2,1)S(1)}, bf16[2,6,144,128]{3,2,1,0:T(8,128)(2,1)S(1)}, u32[]{:S(2)}, u32[]{:S(2)}) %collective-permute-start.4) | collective-permute-done | bytes 442400 | tf_op jit(solution)/shard_map/ppermute | solution.py:489
  352.4 0.1 select_add_fusion.1
  352.5 2.1 collective-permute-start.5
  354.6 32.4 %local_back.1 = (bf16[1024,768]{1,0:T(8,128)(2,1)}, f32[768,128]{1,0:T(8,128)}, f32[1024,1536]{1,0:T(8,128)}, f32[1024,768]{1,0:T(8,128)}) custom-call(s32[2]{0:T(128)} %fusion.split_ref, bf16[1024,1536]{1,0:T(8,128)(2,1)} %get-tuple-element.54.phi_query, bf16[1024,1536]{1,0:T(8,128)(2,1)} %get-tuple-element.51.phi_key, ...), custom_call_target="tpu_custom_call" | custom-call | tf_op jit(solution)/shard_map/local_back/pallas_call | solution.py:457
  387.0 1.0 select_add_fusion.wire
  388.0 16.8 %keys_back.1 = (bf16[1024,768]{1,0:T(8,128)(2,1)}, bf16[1024,768]{1,0:T(8,128)(2,1)}, f32[768,128]{1,0:T(8,128)}) custom-call(s32[2]{0:T(128)} %fusion.split_ref, f32[1024,1536]{1,0:T(8,128)} %get-tuple-element.66.kg, f32[1024,768]{1,0:T(8,128)} %get-tuple-element.67.vg, bf16[1024,1536]{1,0:T(8,128)(2,1)} %get-tuple-element.51.phi_key, ...), custom_call_target="tpu_custom_call" | custom-call | tf_op jit(solution)/shard_map/keys_back/pallas_call | solution.py:457
  404.9 0.5 reduce-scatter.13.cloned.1.call-update
  405.5 5.5 weight_back.3
  411.0 5.6 weight_back.4
  416.7 5.7 weight_back.5
  422.4 4.5 pad_maximum_fusion
  426.9 0.7 reduce-scatter.15.cloned.1.call-update
  427.7 0.7 reduce-scatter.17.cloned.1.call-update
  428.5 10.2 input_back.1
  438.7 0.8 fusion.1
  439.5 37.8 %all-reduce.8 = (f32[2,768]{1,0:T(2,128)S(1)}, f32[2,768]{1,0:T(2,128)S(1)}, f32[2304]{0:T(1024)S(1)}, f32[2,768]{1,0:T(2,128)S(1)}, f32[3072]{0:T(1024)S(1)}) all-reduce(f32[2,768]{1,0:T(2,128)S(1)} %pad_maximum_fusion.1, f32[2,768]{1,0:T(2,128)S(1)} %pad_maximum_fusion.2, ...), channel_id=2, replica_groups=mesh['batch'=4,'seq'=8] {'batch','seq'}, use_global_device_ids=true, to_apply=%region_14.15.clone | all-reduce | flops 9984 | bytes 79872
  477.3 0.6 dynamic-slice.5
  477.9 0.6 dynamic-slice.2
  478.5 0.6 constant_dynamic-slice_fusion.2
  479.1 0.6 constant_dynamic-slice_fusion.1
  479.8 0.6 constant_dynamic-slice_fusion
  480.4 17.0 %reduce-scatter.19.cloned.1.call-done = f32[24,128]{1,0:T(8,128)} async-done(((f32[768,128]{1,0:T(8,128)}), f32[24,128]{1,0:T(8,128)}) %reduce-scatter.19.cloned.1.call-update) | async-done | bytes 12304
  497.4 104.7 %reduce-scatter.13.cloned.1.call-done = f32[24,768]{1,0:T(8,128)} async-done(((f32[768,768]{1,0:T(8,128)}), f32[24,768]{1,0:T(8,128)}) %reduce-scatter.13.cloned.1.call-update) | async-done | bytes 73744 | tf_op jit(solution)/shard_map/reduce_scatter | solution.py:477
  602.1 124.4 %reduce-scatter.11.cloned.1.call-done = f32[24,2304]{1,0:T(8,128)} async-done(((f32[768,2304]{1,0:T(8,128)}), f32[24,2304]{1,0:T(8,128)}) %reduce-scatter.11.cloned.1.call-update) | async-done | bytes 221200 | tf_op jit(solution)/shard_map/reduce_scatter | solution.py:477
  726.5 142.3 %reduce-scatter.15.cloned.1.call-done = f32[24,3072]{1,0:T(8,128)} async-done(((f32[768,3072]{1,0:T(8,128)}), f32[24,3072]{1,0:T(8,128)}) %reduce-scatter.15.cloned.1.call-update) | async-done | bytes 294928 | tf_op jit(solution)/shard_map/reduce_scatter | solution.py:477
  868.8 141.1 %reduce-scatter.17.cloned.1.call-done = f32[96,768]{1,0:T(8,128)} async-done(((f32[3072,768]{1,0:T(8,128)}), f32[96,768]{1,0:T(8,128)}) %reduce-scatter.17.cloned.1.call-update) | async-done | bytes 294928 | tf_op jit(solution)/shard_map/reduce_scatter | solution.py:477
  (55 shorter events, 1.2 us)
Async XLA Ops:
  7.2 207.9 %all-gather.8.cloned.1.call-start = ((), (), s32[]{:S(2)}) async-start(), calls=%async_computation.5 | async-start | bytes 3649536 | tf_op jit(solution)/shard_map/all_gather | solution.py:473
  7.9 264.9 %all-gather.10.cloned.1.call-start = ((), (), s32[]{:S(2)}) async-start(), calls=%async_computation.6 | async-start | bytes 1216512 | tf_op jit(solution)/shard_map/all_gather | solution.py:473
  8.7 273.6 %all-gather.12.cloned.1.call-start = ((), (), s32[]{:S(2)}) async-start(), calls=%async_computation.7 | async-start | bytes 4866048 | tf_op jit(solution)/shard_map/all_gather | solution.py:473
  9.4 272.9 %all-gather.14.cloned.1.call-start = ((), (), s32[]{:S(2)}) async-start(), calls=%async_computation.8 | async-start | bytes 4866048 | tf_op jit(solution)/shard_map/all_gather | solution.py:473
  10.0 487.4 %reduce-scatter.19.cloned.1.call-start = ((), (), s32[]{:S(2)}) async-start(), calls=%async_computation.13 | async-start | bytes 405504
  230.6 2.1 collective-permute-start
  233.8 16.4 %collective-permute-start.1 = (bf16[2,6,144,128]{3,2,1,0:T(8,128)(2,1)S(1)}, bf16[2,6,144,128]{3,2,1,0:T(8,128)(2,1)S(1)}, u32[]{:S(2)}, u32[]{:S(2)}) collective-permute-start(bf16[2,6,144,128]{3,2,1,0:T(8,128)(2,1)S(1)} %select_add_fusion.5), channel_id=1, source_target_pairs={{0,2},{1,3},{2,0},{3,1},{4,6},{5,7},{6,4},{7,5},{8,10},{9,11},{10,... | collective-permute-start | bytes 1327112 | tf_op jit(solution)/shard_map/ppermute | solution.py:489
  250.4 21.5 %collective-permute-start.2 = (bf16[2,6,144,128]{3,2,1,0:T(8,128)(2,1)S(1)}, bf16[2,6,144,128]{3,2,1,0:T(8,128)(2,1)S(1)}, u32[]{:S(2)}, u32[]{:S(2)}) collective-permute-start(bf16[2,6,144,128]{3,2,1,0:T(8,128)(2,1)S(1)} %select_add_fusion.4), channel_id=1, source_target_pairs={{0,4},{1,5},{2,6},{3,7},{4,0},{5,1},{6,2},{7,3},{8,12},{9,13},{10,... | collective-permute-start | bytes 1327112 | tf_op jit(solution)/shard_map/ppermute | solution.py:489
  336.1 2.1 collective-permute-start.3
  339.3 13.0 %collective-permute-start.4 = (bf16[2,6,144,128]{3,2,1,0:T(8,128)(2,1)S(1)}, bf16[2,6,144,128]{3,2,1,0:T(8,128)(2,1)S(1)}, u32[]{:S(2)}, u32[]{:S(2)}) collective-permute-start(bf16[2,6,144,128]{3,2,1,0:T(8,128)(2,1)S(1)} %select_add_fusion.2), channel_id=1, source_target_pairs={{0,2},{1,3},{2,0},{3,1},{4,6},{5,7},{6,4},{7,5},{8,10},{9,11},{10,... | collective-permute-start | bytes 1327112 | tf_op jit(solution)/shard_map/ppermute | solution.py:489
  352.5 34.5 %collective-permute-start.5 = (bf16[2,6,144,128]{3,2,1,0:T(8,128)(2,1)S(1)}, bf16[2,6,144,128]{3,2,1,0:T(8,128)(2,1)S(1)}, u32[]{:S(2)}, u32[]{:S(2)}) collective-permute-start(bf16[2,6,144,128]{3,2,1,0:T(8,128)(2,1)S(1)} %select_add_fusion.1), channel_id=1, source_target_pairs={{0,4},{1,5},{2,6},{3,7},{4,0},{5,1},{6,2},{7,3},{8,12},{9,13},{10,... | collective-permute-start | bytes 1327112 | tf_op jit(solution)/shard_map/ppermute | solution.py:489
  404.8 197.2 %reduce-scatter.13.cloned.1.call-start = ((), (), s32[]{:S(2)}) async-start(), calls=%async_computation.10 | async-start | bytes 2433024 | tf_op jit(solution)/shard_map/reduce_scatter | solution.py:477
  405.4 321.1 %reduce-scatter.11.cloned.1.call-start = ((), (), s32[]{:S(2)}) async-start(), calls=%async_computation.9 | async-start | bytes 7299072 | tf_op jit(solution)/shard_map/reduce_scatter | solution.py:477
  411.0 11.4 %copy-start = (f32[768,768]{1,0:T(8,128)S(1)}, f32[768,768]{1,0:T(8,128)}, u32[]{:S(2)}) copy-start(f32[768,768]{1,0:T(8,128)} %get-tuple-element.77) | copy-start | bytes 7077892
  416.6 5.7 copy-start.1
  426.9 442.0 %reduce-scatter.15.cloned.1.call-start = ((), (), s32[]{:S(2)}) async-start(), calls=%async_computation.11 | async-start | bytes 9732096 | tf_op jit(solution)/shard_map/reduce_scatter | solution.py:477
  427.6 582.3 %reduce-scatter.17.cloned.1.call-start = ((), (), s32[]{:S(2)}) async-start(), calls=%async_computation.12 | async-start | bytes 9732096 | tf_op jit(solution)/shard_map/reduce_scatter | solution.py:477
  427.7 0.7 copy-start.3
  428.4 10.2 %copy-start.4 = (f32[1,768]{1,0:T(1,128)S(1)}, f32[1,768]{1,0:T(1,128)}, u32[]{:S(2)}) copy-start(f32[1,768]{1,0:T(1,128)} %get-tuple-element.80) | copy-start | bytes 9220
  428.4 10.2 %copy-start.5 = (f32[1,768]{1,0:T(1,128)S(1)}, f32[1,768]{1,0:T(1,128)}, u32[]{:S(2)}) copy-start(f32[1,768]{1,0:T(1,128)} %get-tuple-element.81) | copy-start | bytes 9220
  428.4 10.2 %copy-start.6 = (f32[1,768]{1,0:T(1,128)S(1)}, f32[1,768]{1,0:T(1,128)}, u32[]{:S(2)}) copy-start(f32[1,768]{1,0:T(1,128)} %get-tuple-element.82) | copy-start | bytes 9220
  428.5 11.1 %copy-start.2 = (f32[1,3072]{1,0:T(1,128)S(1)}, f32[1,3072]{1,0:T(1,128)}, u32[]{:S(2)}) copy-start(f32[1,3072]{1,0:T(1,128)} %get-tuple-element.86) | copy-start | bytes 36868
Sparse Core Ops, SparseCore 0:
  10.9 62.8 all-gather.7
  76.7 52.8 all-gather.9
  132.5 63.1 all-gather.11
  198.5 70.4 all-gather.13
  405.0 92.3 reduce-scatter.18
  504.0 98.0 reduce-scatter.12
  608.3 118.1 reduce-scatter.10
  734.0 134.8 reduce-scatter.14
  875.3 134.5 reduce-scatter.16
